TPU v7x, 32 devices: a whole 2x2x4 slice. The times are simulated.
32 devices in a mesh: grp: 4 (over x, core), tp: 4 (over z), ex: 2 (over y).
Axes of the slice: x: 2, y: 2, z: 4, core: 2. Of those that a mesh axis runs over, the one named last changes fastest.
Arguments:
- tokens: bfloat16 [128, 7168], P(('grp', 'tp'), 'ex'), may hold values from -6 to 6
- expert_ids: int32 [128, 1], P(('grp', 'tp')), may hold values from 0 to 1; in each aligned block of 8 rows (0 to 7, 8 to 15, ...) at most 6 rows name the same one
- gate_levels: int32 [128, 1], P(('grp', 'tp')), may hold values from 1 to 4095
- gate_weight: bfloat16 [4, 7168, 1024], P('grp', 'ex', 'tp'), may hold values from -0.0625 to 0.0625
- up_weight: bfloat16 [4, 7168, 1024], P('grp', 'ex', 'tp'), may hold values from -0.0625 to 0.0625
- down_weight: bfloat16 [4, 1024, 7168], P('grp', 'tp', 'ex'), may hold values from -0.125 to 0.125
Outputs:
- mixed: bfloat16 [128, 7168], P(('grp', 'tp'), 'ex')
Inputs may be any that keep to these rules, and one draw needn't show every extreme that they name: `expert_ids`: each row names 1 different experts. In each aligned block of 8 rows (the tokens of one index pair of grp and tp) no expert is named by more than 6 rows.
All inputs are finite; a program needn't handle non-finite values.
Results may differ from a plain program's by a relative error of at most 0.0057.
Values may be sent and summed in bfloat16 or wider, within the bound.
No kernel may reach another device: no remote copies, remote signals or barrier semaphores. Data moves between devices by JAX's collectives and lax.ppermute only.
A program may use at most 64 MiB of HBM per device.

v0:
```python
import jax
import jax.numpy as jnp
from jax import lax
from jax.sharding import PartitionSpec as P

ROUTED_SCALE = 2.5


def both_products(rows, w_gate, w_up):
    gate = jnp.dot(rows, w_gate, preferred_element_type=jnp.float32)
    up = jnp.dot(rows, w_up, preferred_element_type=jnp.float32)
    return jnp.concatenate([gate, up], axis=1)


def activate(summed, inner):
    return (jax.nn.silu(summed[:, :inner]) * summed[:, inner:]).astype(jnp.bfloat16)


def per_device(tokens, expert_ids, gate_levels, gate_weight, up_weight, down_weight):
    groups = lax.axis_size("grp")
    experts = groups // 2
    count, width = tokens.shape
    top = expert_ids.shape[1]
    capacity = max(2, 3 * count * top // (2 * experts))
    slots = experts * capacity
    flat = expert_ids.reshape(-1)
    picks_total = flat.shape[0]
    same = flat[:, None] == flat[None, :]
    order = jnp.arange(picks_total, dtype=jnp.int32)
    earlier = order[None, :] < order[:, None]
    rank = jnp.sum(jnp.logical_and(same, earlier), axis=1)
    target = flat * capacity + rank
    onehot = (target[:, None] == jnp.arange(slots, dtype=jnp.int32)[None, :]).astype(jnp.float32)
    onehot = onehot.reshape(count, top, slots)
    placing = jnp.sum(onehot, axis=1).astype(jnp.bfloat16)
    levels = gate_levels.astype(jnp.float32)
    weights = ROUTED_SCALE * levels / jnp.sum(levels, axis=1, keepdims=True)
    mixing = jnp.sum(onehot * weights[:, :, None], axis=1)
    outgoing = jnp.dot(placing.T, tokens, preferred_element_type=jnp.float32).astype(jnp.bfloat16)
    outgoing = outgoing.reshape(experts, 1, capacity, width)
    outgoing = jnp.broadcast_to(outgoing, (experts, 2, capacity, width)).reshape(
        groups, capacity, width
    )
    w_gate = gate_weight[0]
    w_up = up_weight[0]
    w_down = down_weight[0]
    inner = w_gate.shape[1]
    arrived = lax.all_to_all(outgoing, "grp", split_axis=0, concat_axis=0, tiled=True).reshape(
        -1, width
    )
    partial_value = both_products(lax.all_gather(arrived, "tp", axis=0, tiled=True), w_gate, w_up)
    shared = lax.psum_scatter(partial_value, "ex", scatter_dimension=0, tiled=True)
    hidden = lax.all_gather(activate(shared, inner), "ex", axis=0, tiled=True)
    returned = lax.psum_scatter(
        jnp.dot(hidden, w_down, preferred_element_type=jnp.float32),
        "tp",
        scatter_dimension=0,
        tiled=True,
    )
    back = lax.all_to_all(
        returned.reshape(groups, capacity, width), "grp", split_axis=0, concat_axis=0, tiled=True
    )
    halves = back.reshape(experts, 2, capacity, width)
    expert_out = (halves[:, 0] + halves[:, 1]).astype(jnp.bfloat16)
    mixed = jnp.dot(
        mixing,
        expert_out.reshape(slots, width).astype(jnp.float32),
        precision=lax.Precision.HIGHEST,
    )
    return mixed.astype(jnp.bfloat16)


def solution(mesh):
    return jax.shard_map(
        per_device,
        mesh=mesh,
        in_specs=(
            P(("grp", "tp"), "ex"),
            P(("grp", "tp"), None),
            P(("grp", "tp"), None),
            P("grp", "ex", "tp"),
            P("grp", "ex", "tp"),
            P("grp", "tp", "ex"),
        ),
        out_specs=P(("grp", "tp"), "ex"),
        check_vma=False,
    )
```

profile of v0, /device:TPU:0, one launch (start us, length us, event | category | flops | bytes accessed | tf_op | source)
XLA Modules:
  0.0 111.7 jit_solution(5777648908865100098)
XLA Ops:
  6.5 0.0 copy-start
  6.5 0.0 reduce-scatter.3.cloned.1.call-start
  6.5 1.0 convert_reduce_fusion
  7.5 0.7 fusion.17
  8.2 1.1 convolution_convert_fusion
  9.4 9.7 %all_to_all.10 = bf16[4,6,3584]{2,1,0:T(8,128)(2,1)S(1)} all-to-all(bf16[4,6,3584]{2,1,0:T(8,128)(2,1)S(1)} %bitcast.41), channel_id=1, replica_groups=mesh['grp'=4,'tp'=4,'ex'=2] {'grp'}, dimensions={0} | all-to-all | bytes 344064 | tf_op jit(solution)/shard_map/all_to_all | solution.py:48
  19.1 0.1 reshape.112
  19.1 0.0 copy-start.1
  19.1 18.7 %all_gather.6 = bf16[96,3584]{1,0:T(8,128)(2,1)S(1)} all-gather(bf16[24,3584]{1,0:T(8,128)(2,1)S(1)} %reshape.112), channel_id=1, replica_groups=mesh['grp'=4,'tp'=4,'ex'=2] {'tp'}, dimensions={0}, use_global_device_ids=true | all-gather | bytes 860160 | tf_op jit(solution)/shard_map/all_gather | solution.py:51
  37.8 1.9 %fusion.2 = f32[96,256]{1,0:T(8,128)S(1)} fusion(bf16[96,3584]{1,0:T(8,128)(2,1)S(1)} %all_gather.6, bf16[1,3584,256]{2,1,0:T(8,128)(2,1)} %param.10), kind=kOutput, calls=%fused_computation.4 | convolution fusion | flops 176160768 | bytes 2621440 | tf_op jit(solution)/shard_map/dot_general | solution.py:11
  39.8 0.0 copy-done.1
  39.8 0.4 fusion.4
  40.2 0.7 pad_maximum_fusion
  40.9 0.0 reduce-scatter.3.cloned.1.call-update
  40.9 0.0 reduce-scatter.5.cloned.1.call-start
  41.0 10.2 %reduce-scatter.3.cloned.1.call-done = f32[48,512]{1,0:T(8,128)} async-done(((f32[96,512]{1,0:T(8,128)}), f32[48,512]{1,0:T(8,128)}) %reduce-scatter.3.cloned.1.call-update) | async-done | bytes 98320 | tf_op jit(solution)/shard_map/reduce_scatter | solution.py:52
  51.2 0.8 fusion.8
  52.0 4.5 %all_gather.7 = bf16[96,256]{1,0:T(8,128)(2,1)S(1)} all-gather(bf16[48,256]{1,0:T(8,128)(2,1)S(1)} %fusion.8), channel_id=1, replica_groups=mesh['grp'=4,'tp'=4,'ex'=2] {'ex'}, dimensions={0}, use_global_device_ids=true | all-gather | bytes 73728 | tf_op jit(solution)/shard_map/all_gather | solution.py:53
  56.5 0.0 copy-done
  56.6 1.5 %fusion = f32[96,3584]{1,0:T(8,128)} fusion(bf16[96,256]{1,0:T(8,128)(2,1)S(1)} %all_gather.7, bf16[1,256,3584]{2,1,0:T(8,128)(2,1)S(1)} %copy-done), kind=kOutput, calls=%fused_computation.2 | convolution fusion | flops 176160768 | bytes 3260416 | tf_op jit(solution)/shard_map/dot_general | solution.py:55
  58.1 0.0 copy-start.2
  58.1 0.0 reduce-scatter.5.cloned.1.call-update
  58.1 32.4 %reduce-scatter.5.cloned.1.call-done = f32[24,3584]{1,0:T(8,128)} async-done(((f32[96,3584]{1,0:T(8,128)}), f32[24,3584]{1,0:T(8,128)}) %reduce-scatter.5.cloned.1.call-update) | async-done | bytes 344080 | tf_op jit(solution)/shard_map/reduce_scatter | solution.py:54
  90.5 1.8 %reshape.113 = f32[4,6,3584]{2,1,0:T(8,128)} reshape(f32[24,3584]{1,0:T(8,128)} %reduce-scatter.5.cloned.1.call-done) | data formatting | bytes 688128 | tf_op jit(solution)/shard_map/reshape | solution.py:61
  92.3 3.5 %all-to-all-start.1 = ((f32[4,6,3584]{2,1,0:T(8,128)}), f32[4,6,3584]{2,1,0:T(8,128)S(1)}, u32[]{:S(2)}, u32[]{:S(2)}) async-start(f32[4,6,3584]{2,1,0:T(8,128)} %reshape.113), calls=%async_computation.3 | async-start | bytes 917504 | tf_op jit(solution)/shard_map/all_to_all | solution.py:60
  95.8 0.0 copy-done.2
  95.8 8.1 %all-to-all-done.1 = f32[4,6,3584]{2,1,0:T(8,128)S(1)} async-done(((f32[4,6,3584]{2,1,0:T(8,128)}), f32[4,6,3584]{2,1,0:T(8,128)S(1)}, u32[]{:S(2)}, u32[]{:S(2)}) %all-to-all-start.1) | async-done | bytes 344096 | tf_op jit(solution)/shard_map/all_to_all | solution.py:60
  104.0 0.9 convolution_convert_fusion.1
  (5 shorter events, 0.1 us)
Async XLA Ops:
  6.5 50.0 %copy-start = (bf16[1,256,3584]{2,1,0:T(8,128)(2,1)S(1)}, bf16[1,256,3584]{2,1,0:T(8,128)(2,1)}, u32[]{:S(2)}) copy-start(bf16[1,256,3584]{2,1,0:T(8,128)(2,1)} %param.11) | copy-start | bytes 5505028
  6.5 44.7 %reduce-scatter.3.cloned.1.call-start = ((), (), s32[]{:S(2)}) async-start(), calls=%async_computation.4 | async-start | bytes 294912 | tf_op jit(solution)/shard_map/reduce_scatter | solution.py:52
  19.1 20.6 %copy-start.1 = (bf16[1,3584,256]{2,1,0:T(8,128)(2,1)S(1)}, bf16[1,3584,256]{2,1,0:T(8,128)(2,1)}, u32[]{:S(2)}) copy-start(bf16[1,3584,256]{2,1,0:T(8,128)(2,1)} %param.9) | copy-start | bytes 5505028
  40.9 49.6 %reduce-scatter.5.cloned.1.call-start = ((), (), s32[]{:S(2)}) async-start(), calls=%async_computation.5 | async-start | bytes 1720320 | tf_op jit(solution)/shard_map/reduce_scatter | solution.py:54
  58.1 37.7 %copy-start.2 = (s32[8,1]{0,1:T(1,128)S(1)}, s32[8,1]{0,1:T(1,128)}, u32[]{:S(2)}) copy-start(s32[8,1]{0,1:T(1,128)} %param.8) | copy-start | bytes 100
  92.3 11.6 %all-to-all-start.1 = ((f32[4,6,3584]{2,1,0:T(8,128)}), f32[4,6,3584]{2,1,0:T(8,128)S(1)}, u32[]{:S(2)}, u32[]{:S(2)}) async-start(f32[4,6,3584]{2,1,0:T(8,128)} %reshape.113), calls=%async_computation.3 | async-start | bytes 917504 | tf_op jit(solution)/shard_map/all_to_all | solution.py:60
Sparse Core Ops, SparseCore 0:
  41.0 10.1 reduce-scatter.2
  58.2 32.2 reduce-scatter.4
where the time goes:
time: 112 us
  waiting for transfers between devices  50.8 us (45%)
  blocking collectives  32.9 us (29%)
  between operations  13.5 us (12%)
  matrix products  5.88 us (5%)
  starting transfers between devices  3.51 us (3%)
  other arithmetic  3.21 us (3%)
  local copies, waits for them, and re-layouts  1.96 us (2%)
    reduce_scatter x1, waiting for transfers between devices, per_device(): lax.psum_scatter(jnp.dot(hidden, w_down, preferred_element_type=jnp.float...  32.4 us
    all_gather x1, blocking collectives, per_device(): lax.all_gather(arrived, 'tp', axis=0, tiled=True)  18.7 us
    reduce_scatter x1, waiting for transfers between devices, per_device(): lax.psum_scatter(partial_value, 'ex', scatter_dimension=0, tiled=True)  10.2 us
    all_to_all x1, blocking collectives, per_device(): lax.all_to_all(outgoing, 'grp', split_axis=0, concat_axis=0, tiled=True)  9.7 us
    all_to_all x1, waiting for transfers between devices, per_device(): lax.all_to_all(returned.reshape(groups, capacity, width), 'grp', split_ax...  8.09 us
    all_gather x1, blocking collectives, per_device(): hidden = lax.all_gather(activate(shared, inner), 'ex', axis=0, tiled=True)  4.5 us
    all_to_all x1, starting transfers between devices, per_device(): lax.all_to_all(returned.reshape(groups, capacity, width), 'grp', split_ax...  3.46 us
  transfers between devices with their start and end apart: 3, of which 3 were waited for; matrix products, arithmetic and copies ran while one was open for 0% of the time, Pallas kernels for 0%

commit v1 on v0

v1 whole, which is shorter than its diff:
```python
import jax
import jax.numpy as jnp
from jax import lax
from jax.sharding import PartitionSpec as P

ROUTED_SCALE = 2.5
LANES = 128
BASE = 64


def pack(tokens, expert_ids, gate_levels):
    high = gate_levels // BASE
    routing = jnp.concatenate([expert_ids, high, gate_levels - high * BASE], axis=1)
    spare = -routing.shape[1] % LANES
    routing = jnp.pad(routing, ((0, 0), (0, spare))).astype(tokens.dtype)
    return jnp.concatenate([tokens, routing], axis=1)


def weight_of(routing, top, expert):
    routing = routing.astype(jnp.float32)
    ids = routing[:, :top]
    levels = routing[:, top : 2 * top] * BASE + routing[:, 2 * top : 3 * top]
    mine = jnp.where(ids == expert.astype(jnp.float32), levels, 0.0)
    return ROUTED_SCALE * jnp.sum(mine, axis=1, keepdims=True) / jnp.sum(levels, axis=1, keepdims=True)


def shift(value, axis, by):
    size = lax.axis_size(axis)
    return lax.ppermute(value, axis, [(i, (i + by) % size) for i in range(size)])


def shift_expert(value, by):
    groups = lax.axis_size("grp")
    return lax.ppermute(value, "grp", [(i, (i + 2 * by) % groups) for i in range(groups)])


def swap_half(value):
    return lax.ppermute(value, "grp", [(i, i ^ 1) for i in range(lax.axis_size("grp"))])


def per_device(tokens, expert_ids, gate_levels, gate_weight, up_weight, down_weight):
    bf16, f32 = jnp.bfloat16, jnp.float32
    experts = lax.axis_size("grp") // 2
    n_tp, n_ex = lax.axis_size("tp"), lax.axis_size("ex")
    count, width = tokens.shape
    top = expert_ids.shape[1]
    expert = lax.axis_index("grp") // 2
    w_both = (gate_weight[0], up_weight[0])
    w_down = down_weight[0]
    inner = w_down.shape[0]

    own = pack(tokens, expert_ids, gate_levels)
    line = jnp.concatenate([own] + [shift(own, "tp", s) for s in range(1, n_tp)], axis=0)
    chunks = [line] + [shift_expert(line, s) for s in range(1, experts)]
    sums = []
    for rows in (chunks[0], jnp.concatenate(chunks[1:], axis=0)):
        rows = jnp.concatenate([rows, swap_half(rows)], axis=0)
        scale = weight_of(rows[:, width:], top, expert)
        rows = rows[:, :width]
        part = jnp.concatenate([jnp.dot(rows, w, preferred_element_type=f32) for w in w_both], axis=1)
        sent = part.astype(bf16)
        for s in range(1, n_ex):
            part = part + shift(sent, "ex", s).astype(f32)
        hidden = (jax.nn.silu(part[:, :inner]) * part[:, inner:]).astype(bf16)
        out = jnp.dot(hidden, w_down, preferred_element_type=f32) * scale
        kept = out.shape[0] // 2
        sums.append(out[:kept] + swap_half(out[kept:].astype(bf16)).astype(f32))
    total = sums[0]
    for s in range(1, experts):
        far = lax.slice_in_dim(sums[1], (s - 1) * n_tp * count, s * n_tp * count, axis=0)
        total = total + shift_expert(far.astype(bf16), -s).astype(f32)
    total = total.reshape(n_tp, count, width)
    mixed = total[0]
    for s in range(1, n_tp):
        mixed = mixed + shift(total[s].astype(bf16), "tp", -s).astype(f32)
    return mixed.astype(bf16)


def solution(mesh):
    return jax.shard_map(
        per_device,
        mesh=mesh,
        in_specs=(
            P(("grp", "tp"), "ex"),
            P(("grp", "tp"), None),
            P(("grp", "tp"), None),
            P("grp", "ex", "tp"),
            P("grp", "ex", "tp"),
            P("grp", "tp", "ex"),
        ),
        out_specs=P(("grp", "tp"), "ex"),
        check_vma=False,
    )
```

time: 112 us -> 49.8 us (0.44)
  blocking collectives: 32.9 us -> 0 us
  waiting for transfers between devices: 50.8 us -> 22 us
  starting transfers between devices: 3.51 us -> 18 us
  between operations: 13.5 us -> 0.17 us
  other arithmetic: 3.21 us -> 5 us
  matrix products: 5.88 us -> 4.1 us
  local copies, waits for them, and re-layouts: 1.96 us -> 0.29 us
    reduce_scatter x2 -> x0, waiting for transfers between devices: 42.6 us -> none  [the longest x1 32.4 us: per_device(): lax.psum_scatter(jnp.dot(hidden, w_down, preferred_element_type=jnp.float...]
    all_gather x2 -> x0, blocking collectives: 23.2 us -> none  [the longest x1 18.7 us: per_device(): lax.all_gather(arrived, 'tp', axis=0, tiled=True)]
    ppermute x0 -> x14, waiting for transfers between devices: none -> 22 us  [the longest x8 12.9 us: shift(): lax.ppermute(value, axis, [(i, (i + by) % size) for i in range(size)])]
    ppermute x0 -> x14, starting transfers between devices: none -> 18 us  [the longest x8 15.2 us: shift(): lax.ppermute(value, axis, [(i, (i + by) % size) for i in range(size)])]
    all_to_all x1 -> x0, blocking collectives: 9.7 us -> none  [per_device(): lax.all_to_all(outgoing, 'grp', split_axis=0, concat_axis=0, tiled=True)]
    all_to_all x1 -> x0, waiting for transfers between devices: 8.09 us -> none  [per_device(): lax.all_to_all(returned.reshape(groups, capacity, width), 'grp', split_ax...]
    all_to_all x1 -> x0, starting transfers between devices: 3.46 us -> none  [per_device(): lax.all_to_all(returned.reshape(groups, capacity, width), 'grp', split_ax...]
    another operation x0 -> x4, other arithmetic: none -> 2.19 us
  transfers between devices with their start and end apart: 3 -> 14, of which waited for: 3 -> 9; matrix products, arithmetic and copies ran while one was open for 0% -> 7% of each run, Pallas kernels for 0% -> 0%
where the time goes in v1:
time: 49.8 us; the launch traced here: 49.6 us
  waiting for transfers between devices  22 us (44%)
  starting transfers between devices  18 us (36%)
  other arithmetic  5 us (10%)
  matrix products  4.1 us (8%)
    ppermute x8, starting transfers between devices, shift(): lax.ppermute(value, axis, [(i, (i + by) % size) for i in range(size)])  15.2 us
    ppermute x8, waiting for transfers between devices, shift(): lax.ppermute(value, axis, [(i, (i + by) % size) for i in range(size)])  12.9 us
    ppermute x2, waiting for transfers between devices, shift_expert(): lax.ppermute(value, 'grp', [(i, (i + 2 * by) % groups) for i in range(gro...  7.1 us
    dot_general x4, matrix products, per_device(): jnp.dot(rows, w, preferred_element_type=f32)  3.26 us
    another operation x4, other arithmetic  2.19 us
    ppermute x2, starting transfers between devices, shift_expert(): lax.ppermute(value, 'grp', [(i, (i + 2 * by) % groups) for i in range(gro...  2.15 us
    ppermute x4, waiting for transfers between devices, swap_half(): lax.ppermute(value, 'grp', [(i, i ^ 1) for i in range(lax.axis_size('grp'...  1.93 us
  transfers between devices with their start and end apart: 14, of which 9 were waited for; matrix products, arithmetic and copies ran while one was open for 7% of the time, Pallas kernels for 0%

profile of v1, /device:TPU:0, one launch (start us, length us, event | category | flops | bytes accessed | tf_op | source)
XLA Modules:
  0.0 49.6 jit_solution(10566890436233879766)
XLA Ops:
  0.0 0.0 copy-start
  0.0 0.8 %convert.22 = bf16[8,1]{0,1:T(2,128)(2,1)S(1)} convert(s32[8,1]{0,1:T(1,128)} %param.7) | non-fusion elementwise | flops 8 | bytes 48 | tf_op jit(solution)/shard_map/convert.7
  0.8 0.7 %fusion.33 = (bf16[8,1]{0,1:T(2,128)(2,1)S(1)}, s32[8,1]{0,1:T(1,128)S(1)}) fusion(s32[8,1]{0,1:T(1,128)} %param.8), kind=kLoop, calls=%fused_computation.68 | loop fusion | flops 128 | bytes 80 | tf_op jit(solution)/shard_map/convert.8
  1.5 0.7 %subtract_convert_fusion = bf16[8,1]{0,1:T(2,128)(2,1)S(1)} fusion(s32[8,1]{0,1:T(1,128)} %param.8, s32[8,1]{0,1:T(1,128)S(1)} %get-tuple-element.8), kind=kLoop, calls=%fused_computation.64 | loop fusion | flops 24 | bytes 80 | tf_op jit(solution)/shard_map/convert.9
  2.1 0.1 copy.9
  2.2 0.8 %constant_dynamic-update-slice_fusion.4 = (bf16[64,3712]{1,0:T(8,128)(2,1)S(1)}, bf16[8,3712]{1,0:T(8,128)(2,1)S(1)}) fusion(bf16[8,128]{1,0:T(8,128)(2,1)S(1)} %pad.5.clone, bf16[8,3584]{1,0:T(8,128)(2,1)} %param.6), kind=kLoop, calls=%fused_computation.56 | loop fusion | flops 118783 | bytes 178176
  3.1 4.1 %collective-permute-start.1 = (bf16[8,3712]{1,0:T(8,128)(2,1)S(1)}, bf16[8,3712]{1,0:T(8,128)(2,1)S(1)}, u32[]{:S(2)}, u32[]{:S(2)}) collective-permute-start(bf16[8,3712]{1,0:T(8,128)(2,1)S(1)} %get-tuple-element.13), channel_id=1, source_target_pairs={{0,4},{2,6},{4,0},{6,2},{1,5},{3,7},{5,1},{7,3},{8,12},{10,14},{12... | collective-permute-start | bytes 178184 | tf_op jit(solution)/shard_map/ppermute | solution.py:29
  7.2 1.6 %collective-permute-start = (bf16[8,3712]{1,0:T(8,128)(2,1)S(1)}, bf16[8,3712]{1,0:T(8,128)(2,1)S(1)}, u32[]{:S(2)}, u32[]{:S(2)}) collective-permute-start(bf16[8,3712]{1,0:T(8,128)(2,1)S(1)} %get-tuple-element.13), channel_id=1, source_target_pairs={{0,2},{2,4},{4,6},{6,0},{1,3},{3,5},{5,7},{7,1},{8,10},{10,12},{12... | collective-permute-start | bytes 178184 | tf_op jit(solution)/shard_map/ppermute | solution.py:29
  8.7 2.2 %collective-permute-start.2 = (bf16[8,3712]{1,0:T(8,128)(2,1)S(1)}, bf16[8,3712]{1,0:T(8,128)(2,1)S(1)}, u32[]{:S(2)}, u32[]{:S(2)}) collective-permute-start(bf16[8,3712]{1,0:T(8,128)(2,1)S(1)} %get-tuple-element.13), channel_id=1, source_target_pairs={{0,6},{2,0},{4,2},{6,4},{1,7},{3,1},{5,3},{7,5},{8,14},{10,8},{12,... | collective-permute-start | bytes 178184 | tf_op jit(solution)/shard_map/ppermute | solution.py:29
  11.0 0.0 copy-start.2
  11.0 0.0 collective-permute-done.1
  11.0 2.3 %collective-permute-done = bf16[8,3712]{1,0:T(8,128)(2,1)S(1)} collective-permute-done((bf16[8,3712]{1,0:T(8,128)(2,1)S(1)}, bf16[8,3712]{1,0:T(8,128)(2,1)S(1)}, u32[]{:S(2)}, u32[]{:S(2)}) %collective-permute-start) | collective-permute-done | bytes 59424 | tf_op jit(solution)/shard_map/ppermute | solution.py:29
  13.3 0.3 collective-permute-done.2
  13.6 0.8 %pad_maximum_fusion = bf16[32,3712]{1,0:T(8,128)(2,1)S(1)} fusion(bf16[8,3712]{1,0:T(8,128)(2,1)S(1)} %collective-permute-done.2, bf16[8,3712]{1,0:T(8,128)(2,1)S(1)} %collective-permute-done.1, bf16[8,3712]{1,0:T(8,128)(2,1)S(1)} %collective-permute-done, bf16[8,128]{1,0:T(8,128)(2,1)S(1)} %pad.5.clone, bf16[8,3584]{1,0:T(8,128)(2,1)} %param.6), kind=kLoop, calls=%fused_computation.22 | loop fusion | flops 1187840 | bytes 475136 | tf_op jit(solution)/shard_map/concatenate | solution.py:53
  14.4 1.6 %collective-permute-start.6 = (bf16[32,3712]{1,0:T(8,128)(2,1)S(1)}, bf16[32,3712]{1,0:T(8,128)(2,1)S(1)}, u32[]{:S(2)}, u32[]{:S(2)}) collective-permute-start(bf16[32,3712]{1,0:T(8,128)(2,1)S(1)} %pad_maximum_fusion), channel_id=1, source_target_pairs={{0,16},{8,24},{16,0},{24,8},{1,17},{9,25},{17,1},{25,9},{2,18},{10... | collective-permute-start | bytes 712712 | tf_op jit(solution)/shard_map/ppermute | solution.py:34
  16.0 0.0 collective-permute-start.3
  16.0 1.5 %collective-permute-done.3 = bf16[32,3712]{1,0:T(8,128)(2,1)S(1)} collective-permute-done((bf16[32,3712]{1,0:T(8,128)(2,1)S(1)}, bf16[32,3712]{1,0:T(8,128)(2,1)S(1)}, u32[]{:S(2)}, u32[]{:S(2)}) %collective-permute-start.3) | collective-permute-done | bytes 237600 | tf_op jit(solution)/shard_map/ppermute | solution.py:38
  17.5 1.9 %fusion.4 = f32[64,256]{1,0:T(8,128)S(1)} fusion(bf16[1,3584,256]{2,1,0:T(8,128)(2,1)} %param.10, bf16[64,3712]{1,0:T(8,128)(2,1)S(1)} %constant_dynamic-update-slice_fusion), kind=kOutput, calls=%fused_computation.6 | convolution fusion | flops 117440512 | bytes 2359296 | tf_op jit(solution)/shard_map/dot_general | solution.py:60
  19.4 0.0 copy-done.2
  19.4 0.0 copy-start.1
  19.5 0.4 fusion.8
  19.9 1.6 %collective-permute-start.4 = (bf16[64,512]{1,0:T(8,128)(2,1)S(1)}, bf16[64,512]{1,0:T(8,128)(2,1)S(1)}, u32[]{:S(2)}, u32[]{:S(2)}) collective-permute-start(bf16[64,512]{1,0:T(8,128)(2,1)S(1)} %fusion.20), channel_id=1, source_target_pairs={{0,1},{1,0},{2,3},{3,2},{4,5},{5,4},{6,7},{7,6},{8,9},{9,8},{10,11... | collective-permute-start | bytes 196616 | tf_op jit(solution)/shard_map/ppermute | solution.py:29
  21.5 0.0 collective-permute-done.6
  21.5 0.1 collective-permute-start.7
  21.6 0.2 fusion.27
  21.8 2.4 %collective-permute-done.4 = bf16[64,512]{1,0:T(8,128)(2,1)S(1)} collective-permute-done((bf16[64,512]{1,0:T(8,128)(2,1)S(1)}, bf16[64,512]{1,0:T(8,128)(2,1)S(1)}, u32[]{:S(2)}, u32[]{:S(2)}) %collective-permute-start.4) | collective-permute-done | bytes 65568 | tf_op jit(solution)/shard_map/ppermute | solution.py:29
  24.3 0.0 collective-permute-done.7
  24.3 0.0 copy-done.1
  24.3 0.4 fusion.2
  24.8 0.4 fusion.6
  25.2 1.6 %collective-permute-start.8 = (bf16[64,512]{1,0:T(8,128)(2,1)S(1)}, bf16[64,512]{1,0:T(8,128)(2,1)S(1)}, u32[]{:S(2)}, u32[]{:S(2)}) collective-permute-start(bf16[64,512]{1,0:T(8,128)(2,1)S(1)} %fusion.19), channel_id=1, source_target_pairs={{0,1},{1,0},{2,3},{3,2},{4,5},{5,4},{6,7},{7,6},{8,9},{9,8},{10,11... | collective-permute-start | bytes 196616 | tf_op jit(solution)/shard_map/ppermute | solution.py:29
  26.8 0.2 fusion.28
  27.0 2.6 %collective-permute-done.8 = bf16[64,512]{1,0:T(8,128)(2,1)S(1)} collective-permute-done((bf16[64,512]{1,0:T(8,128)(2,1)S(1)}, bf16[64,512]{1,0:T(8,128)(2,1)S(1)}, u32[]{:S(2)}, u32[]{:S(2)}) %collective-permute-start.8) | collective-permute-done | bytes 65568 | tf_op jit(solution)/shard_map/ppermute | solution.py:29
  29.6 0.0 copy-done
  29.6 0.4 convolution_multiply_fusion
  30.1 0.1 collective-permute-start.9
  30.1 0.4 convolution_multiply_fusion.1
  30.6 0.6 %collective-permute-start.5 = (bf16[32,3584]{1,0:T(8,128)(2,1)S(1)}, bf16[32,3584]{1,0:T(8,128)(2,1)S(1)}, u32[]{:S(2)}, u32[]{:S(2)}) collective-permute-start(bf16[32,3584]{1,0:T(8,128)(2,1)S(1)} %slice.187), channel_id=1, source_target_pairs={{0,8},{8,0},{16,24},{24,16},{1,9},{9,1},{17,25},{25,17},{2,10},{10... | collective-permute-start | bytes 688136 | tf_op jit(solution)/shard_map/ppermute | solution.py:38
  31.2 0.5 collective-permute-done.9
  31.7 0.6 %collective-permute-start.10 = (bf16[32,3584]{1,0:T(8,128)(2,1)S(1)}, bf16[32,3584]{1,0:T(8,128)(2,1)S(1)}, u32[]{:S(2)}, u32[]{:S(2)}) collective-permute-start(bf16[32,3584]{1,0:T(8,128)(2,1)S(1)} %fusion.10), channel_id=1, source_target_pairs={{0,16},{8,24},{16,0},{24,8},{1,17},{9,25},{17,1},{25,9},{2,18},{10... | collective-permute-start | bytes 688136 | tf_op jit(solution)/shard_map/ppermute | solution.py:34
  32.3 0.0 collective-permute-done.5
  32.3 7.1 %collective-permute-done.10 = bf16[32,3584]{1,0:T(8,128)(2,1)S(1)} collective-permute-done((bf16[32,3584]{1,0:T(8,128)(2,1)S(1)}, bf16[32,3584]{1,0:T(8,128)(2,1)S(1)}, u32[]{:S(2)}, u32[]{:S(2)}) %collective-permute-start.10) | collective-permute-done | bytes 229408 | tf_op jit(solution)/shard_map/ppermute | solution.py:34
  39.4 0.1 fusion.31
  39.5 3.5 %collective-permute-start.11 = (bf16[8,3584]{1,0:T(8,128)(2,1)S(1)}, bf16[8,3584]{1,0:T(8,128)(2,1)S(1)}, u32[]{:S(2)}, u32[]{:S(2)}) collective-permute-start(bf16[8,3584]{1,0:T(8,128)(2,1)S(1)} %get-tuple-element.9), channel_id=1, source_target_pairs={{0,6},{2,0},{4,2},{6,4},{1,7},{3,1},{5,3},{7,5},{8,14},{10,8},{12,... | collective-permute-start | bytes 172040 | tf_op jit(solution)/shard_map/ppermute | solution.py:29
  42.9 0.0 collective-permute-start.13
  42.9 0.6 %collective-permute-start.12 = (bf16[8,3584]{1,0:T(8,128)(2,1)S(1)}, bf16[8,3584]{1,0:T(8,128)(2,1)S(1)}, u32[]{:S(2)}, u32[]{:S(2)}) collective-permute-start(bf16[8,3584]{1,0:T(8,128)(2,1)S(1)} %get-tuple-element.11), channel_id=1, source_target_pairs={{0,4},{2,6},{4,0},{6,2},{1,5},{3,7},{5,1},{7,3},{8,12},{10,14},{12... | collective-permute-start | bytes 172040 | tf_op jit(solution)/shard_map/ppermute | solution.py:29
  43.6 1.2 %collective-permute-done.11 = bf16[8,3584]{1,0:T(8,128)(2,1)S(1)} collective-permute-done((bf16[8,3584]{1,0:T(8,128)(2,1)S(1)}, bf16[8,3584]{1,0:T(8,128)(2,1)S(1)}, u32[]{:S(2)}, u32[]{:S(2)}) %collective-permute-start.11) | collective-permute-done | bytes 57376 | tf_op jit(solution)/shard_map/ppermute | solution.py:29
  44.8 4.1 %collective-permute-done.13 = bf16[8,3584]{1,0:T(8,128)(2,1)S(1)} collective-permute-done((bf16[8,3584]{1,0:T(8,128)(2,1)S(1)}, bf16[8,3584]{1,0:T(8,128)(2,1)S(1)}, u32[]{:S(2)}, u32[]{:S(2)}) %collective-permute-start.13) | collective-permute-done | bytes 57376 | tf_op jit(solution)/shard_map/ppermute | solution.py:29
  48.9 0.0 collective-permute-done.12
  48.9 0.7 %fusion.18 = bf16[8,3584]{1,0:T(8,128)(2,1)} fusion(f32[32,3584]{1,0:T(8,128)S(1)} %get-tuple-element.6, bf16[8,3584]{1,0:T(8,128)(2,1)S(1)} %collective-permute-done.13, bf16[8,3584]{1,0:T(8,128)(2,1)S(1)} %collective-permute-done.12, bf16[8,3584]{1,0:T(8,128)(2,1)S(1)} %collective-permute-done.11), kind=kLoop, calls=%fused_computation.30 | loop fusion | flops 200704 | bytes 344064 | tf_op jit(solution)/shard_map/convert_element_type | solution.py:76
  (18 shorter events, 0.3 us)
Async XLA Ops:
  0.0 29.6 %copy-start = (bf16[1,256,3584]{2,1,0:T(8,128)(2,1)S(1)}, bf16[1,256,3584]{2,1,0:T(8,128)(2,1)}, u32[]{:S(2)}) copy-start(bf16[1,256,3584]{2,1,0:T(8,128)(2,1)} %param.11) | copy-start | bytes 5505028
  3.1 7.9 %collective-permute-start.1 = (bf16[8,3712]{1,0:T(8,128)(2,1)S(1)}, bf16[8,3712]{1,0:T(8,128)(2,1)S(1)}, u32[]{:S(2)}, u32[]{:S(2)}) collective-permute-start(bf16[8,3712]{1,0:T(8,128)(2,1)S(1)} %get-tuple-element.13), channel_id=1, source_target_pairs={{0,4},{2,6},{4,0},{6,2},{1,5},{3,7},{5,1},{7,3},{8,12},{10,14},{12... | collective-permute-start | bytes 178184 | tf_op jit(solution)/shard_map/ppermute | solution.py:29
  7.2 6.1 %collective-permute-start = (bf16[8,3712]{1,0:T(8,128)(2,1)S(1)}, bf16[8,3712]{1,0:T(8,128)(2,1)S(1)}, u32[]{:S(2)}, u32[]{:S(2)}) collective-permute-start(bf16[8,3712]{1,0:T(8,128)(2,1)S(1)} %get-tuple-element.13), channel_id=1, source_target_pairs={{0,2},{2,4},{4,6},{6,0},{1,3},{3,5},{5,7},{7,1},{8,10},{10,12},{12... | collective-permute-start | bytes 178184 | tf_op jit(solution)/shard_map/ppermute | solution.py:29
  8.7 4.8 %collective-permute-start.2 = (bf16[8,3712]{1,0:T(8,128)(2,1)S(1)}, bf16[8,3712]{1,0:T(8,128)(2,1)S(1)}, u32[]{:S(2)}, u32[]{:S(2)}) collective-permute-start(bf16[8,3712]{1,0:T(8,128)(2,1)S(1)} %get-tuple-element.13), channel_id=1, source_target_pairs={{0,6},{2,0},{4,2},{6,4},{1,7},{3,1},{5,3},{7,5},{8,14},{10,8},{12,... | collective-permute-start | bytes 178184 | tf_op jit(solution)/shard_map/ppermute | solution.py:29
  11.0 8.5 %copy-start.2 = (bf16[1,3584,256]{2,1,0:T(8,128)(2,1)S(1)}, bf16[1,3584,256]{2,1,0:T(8,128)(2,1)}, u32[]{:S(2)}) copy-start(bf16[1,3584,256]{2,1,0:T(8,128)(2,1)} %param.9) | copy-start | bytes 5505028
  14.4 7.1 %collective-permute-start.6 = (bf16[32,3712]{1,0:T(8,128)(2,1)S(1)}, bf16[32,3712]{1,0:T(8,128)(2,1)S(1)}, u32[]{:S(2)}, u32[]{:S(2)}) collective-permute-start(bf16[32,3712]{1,0:T(8,128)(2,1)S(1)} %pad_maximum_fusion), channel_id=1, source_target_pairs={{0,16},{8,24},{16,0},{24,8},{1,17},{9,25},{17,1},{25,9},{2,18},{10... | collective-permute-start | bytes 712712 | tf_op jit(solution)/shard_map/ppermute | solution.py:34
  16.0 1.5 %collective-permute-start.3 = (bf16[32,3712]{1,0:T(8,128)(2,1)S(1)}, bf16[32,3712]{1,0:T(8,128)(2,1)S(1)}, u32[]{:S(2)}, u32[]{:S(2)}) collective-permute-start(bf16[32,3712]{1,0:T(8,128)(2,1)S(1)} %pad_maximum_fusion), channel_id=1, source_target_pairs={{0,8},{8,0},{16,24},{24,16},{1,9},{9,1},{17,25},{25,17},{2,10},{10... | collective-permute-start | bytes 712712 | tf_op jit(solution)/shard_map/ppermute | solution.py:38
  19.4 4.9 %copy-start.1 = (bf16[1,3584,256]{2,1,0:T(8,128)(2,1)S(1)}, bf16[1,3584,256]{2,1,0:T(8,128)(2,1)}, u32[]{:S(2)}) copy-start(bf16[1,3584,256]{2,1,0:T(8,128)(2,1)} %param.10) | copy-start | bytes 5505028
  19.9 4.3 %collective-permute-start.4 = (bf16[64,512]{1,0:T(8,128)(2,1)S(1)}, bf16[64,512]{1,0:T(8,128)(2,1)S(1)}, u32[]{:S(2)}, u32[]{:S(2)}) collective-permute-start(bf16[64,512]{1,0:T(8,128)(2,1)S(1)} %fusion.20), channel_id=1, source_target_pairs={{0,1},{1,0},{2,3},{3,2},{4,5},{5,4},{6,7},{7,6},{8,9},{9,8},{10,11... | collective-permute-start | bytes 196616 | tf_op jit(solution)/shard_map/ppermute | solution.py:29
  21.5 2.8 %collective-permute-start.7 = (bf16[32,3712]{1,0:T(8,128)(2,1)S(1)}, bf16[32,3712]{1,0:T(8,128)(2,1)S(1)}, u32[]{:S(2)}, u32[]{:S(2)}) collective-permute-start(bf16[32,3712]{1,0:T(8,128)(2,1)S(1)} %collective-permute-done.6), channel_id=1, source_target_pairs={{0,8},{8,0},{16,24},{24,16},{1,9},{9,1},{17,25},{25,17},{2,10},{10... | collective-permute-start | bytes 712712 | tf_op jit(solution)/shard_map/ppermute | solution.py:38
  25.2 4.3 %collective-permute-start.8 = (bf16[64,512]{1,0:T(8,128)(2,1)S(1)}, bf16[64,512]{1,0:T(8,128)(2,1)S(1)}, u32[]{:S(2)}, u32[]{:S(2)}) collective-permute-start(bf16[64,512]{1,0:T(8,128)(2,1)S(1)} %fusion.19), channel_id=1, source_target_pairs={{0,1},{1,0},{2,3},{3,2},{4,5},{5,4},{6,7},{7,6},{8,9},{9,8},{10,11... | collective-permute-start | bytes 196616 | tf_op jit(solution)/shard_map/ppermute | solution.py:29
  30.1 1.6 %collective-permute-start.9 = (bf16[32,3584]{1,0:T(8,128)(2,1)S(1)}, bf16[32,3584]{1,0:T(8,128)(2,1)S(1)}, u32[]{:S(2)}, u32[]{:S(2)}) collective-permute-start(bf16[32,3584]{1,0:T(8,128)(2,1)S(1)} %slice.186), channel_id=1, source_target_pairs={{0,8},{8,0},{16,24},{24,16},{1,9},{9,1},{17,25},{25,17},{2,10},{10... | collective-permute-start | bytes 688136 | tf_op jit(solution)/shard_map/ppermute | solution.py:38
  30.6 1.7 %collective-permute-start.5 = (bf16[32,3584]{1,0:T(8,128)(2,1)S(1)}, bf16[32,3584]{1,0:T(8,128)(2,1)S(1)}, u32[]{:S(2)}, u32[]{:S(2)}) collective-permute-start(bf16[32,3584]{1,0:T(8,128)(2,1)S(1)} %slice.187), channel_id=1, source_target_pairs={{0,8},{8,0},{16,24},{24,16},{1,9},{9,1},{17,25},{25,17},{2,10},{10... | collective-permute-start | bytes 688136 | tf_op jit(solution)/shard_map/ppermute | solution.py:38
  31.7 7.7 %collective-permute-start.10 = (bf16[32,3584]{1,0:T(8,128)(2,1)S(1)}, bf16[32,3584]{1,0:T(8,128)(2,1)S(1)}, u32[]{:S(2)}, u32[]{:S(2)}) collective-permute-start(bf16[32,3584]{1,0:T(8,128)(2,1)S(1)} %fusion.10), channel_id=1, source_target_pairs={{0,16},{8,24},{16,0},{24,8},{1,17},{9,25},{17,1},{25,9},{2,18},{10... | collective-permute-start | bytes 688136 | tf_op jit(solution)/shard_map/ppermute | solution.py:34
  39.5 5.3 %collective-permute-start.11 = (bf16[8,3584]{1,0:T(8,128)(2,1)S(1)}, bf16[8,3584]{1,0:T(8,128)(2,1)S(1)}, u32[]{:S(2)}, u32[]{:S(2)}) collective-permute-start(bf16[8,3584]{1,0:T(8,128)(2,1)S(1)} %get-tuple-element.9), channel_id=1, source_target_pairs={{0,6},{2,0},{4,2},{6,4},{1,7},{3,1},{5,3},{7,5},{8,14},{10,8},{12,... | collective-permute-start | bytes 172040 | tf_op jit(solution)/shard_map/ppermute | solution.py:29
  42.9 6.0 %collective-permute-start.13 = (bf16[8,3584]{1,0:T(8,128)(2,1)S(1)}, bf16[8,3584]{1,0:T(8,128)(2,1)S(1)}, u32[]{:S(2)}, u32[]{:S(2)}) collective-permute-start(bf16[8,3584]{1,0:T(8,128)(2,1)S(1)} %get-tuple-element.10), channel_id=1, source_target_pairs={{0,2},{2,4},{4,6},{6,0},{1,3},{3,5},{5,7},{7,1},{8,10},{10,12},{12... | collective-permute-start | bytes 172040 | tf_op jit(solution)/shard_map/ppermute | solution.py:29
  42.9 6.0 %collective-permute-start.12 = (bf16[8,3584]{1,0:T(8,128)(2,1)S(1)}, bf16[8,3584]{1,0:T(8,128)(2,1)S(1)}, u32[]{:S(2)}, u32[]{:S(2)}) collective-permute-start(bf16[8,3584]{1,0:T(8,128)(2,1)S(1)} %get-tuple-element.11), channel_id=1, source_target_pairs={{0,4},{2,6},{4,0},{6,2},{1,5},{3,7},{5,1},{7,3},{8,12},{10,14},{12... | collective-permute-start | bytes 172040 | tf_op jit(solution)/shard_map/ppermute | solution.py:29

commit v2 on v1

v2 whole, which is shorter than its diff:
```python
import functools

import jax
import jax.numpy as jnp
from jax import lax
from jax.experimental import pallas as pl
from jax.experimental.pallas import tpu as pltpu
from jax.sharding import PartitionSpec as P

ROUTED_SCALE = 2.5
MIB = 1024 * 1024


def shift(value, axis, by):
    size = lax.axis_size(axis)
    return lax.ppermute(value, axis, [(i, (i + by) % size) for i in range(size)])


def shift_expert(value, by_expert, by_tp=0):
    groups, n_tp = lax.axis_size("grp"), lax.axis_size("tp")
    pairs = []
    for g in range(groups):
        for t in range(n_tp):
            to = (g + 2 * by_expert) % groups * n_tp + (t + by_tp) % n_tp
            pairs.append((g * n_tp + t, to))
    return lax.ppermute(value, ("grp", "tp"), pairs)


def swap_half(value):
    return lax.ppermute(value, "grp", [(i, i ^ 1) for i in range(lax.axis_size("grp"))])


def hand_on(*refs):
    del refs


def after(value, *earlier):
    return pl.pallas_call(
        hand_on,
        out_shape=jax.ShapeDtypeStruct(value.shape, value.dtype),
        in_specs=[pl.BlockSpec(memory_space=pl.ANY)] * (1 + len(earlier)),
        out_specs=pl.BlockSpec(memory_space=pl.ANY),
        input_output_aliases={0: 0},
        compiler_params=pltpu.CompilerParams(vmem_limit_bytes=MIB),
    )(value, *earlier)


def copy_kernel(from_ref, to_ref):
    to_ref[...] = from_ref[...]


def copied(value):
    return pl.pallas_call(
        copy_kernel,
        out_shape=jax.ShapeDtypeStruct(value.shape, value.dtype),
        compiler_params=pltpu.CompilerParams(vmem_limit_bytes=2 * MIB),
    )(value)


def mix_kernel(n_tp, experts, ids_ref, levels_ref, *refs):
    *piece_refs, mixed_ref = refs
    count = mixed_ref.shape[0]
    expert = lax.axis_index("grp") // 2
    row = lax.broadcasted_iota(jnp.int32, (count, count), 0)
    column = lax.broadcasted_iota(jnp.int32, (count, count), 1)
    ids = ids_ref[...]
    levels = levels_ref[...].astype(jnp.float32)
    whole = jnp.sum(levels, axis=0, keepdims=True)
    mixed = jnp.zeros(mixed_ref.shape, jnp.float32)
    for s in range(experts):
        source = lax.rem(expert - s + experts, experts)
        weight = ROUTED_SCALE * jnp.sum(jnp.where(ids == source, levels, 0.0), axis=0, keepdims=True) / whole
        upright = jnp.sum(jnp.where(row == column, weight, 0.0), axis=1, keepdims=True)
        total = piece_refs[s * n_tp][...].astype(jnp.float32)
        for t in range(1, n_tp):
            total = total + piece_refs[s * n_tp + t][...].astype(jnp.float32)
        mixed = mixed + upright * total.astype(jnp.bfloat16).astype(jnp.float32)
    mixed_ref[...] = mixed.astype(mixed_ref.dtype)


def mix(expert_ids, gate_levels, pieces, n_tp, experts):
    return pl.pallas_call(
        functools.partial(mix_kernel, n_tp, experts),
        out_shape=jax.ShapeDtypeStruct(pieces[0].shape, jnp.bfloat16),
        compiler_params=pltpu.CompilerParams(vmem_limit_bytes=12 * MIB),
    )(expert_ids.T, gate_levels.T, *pieces)


def per_device(tokens, expert_ids, gate_levels, gate_weight, up_weight, down_weight):
    bf16, f32 = jnp.bfloat16, jnp.float32
    experts = lax.axis_size("grp") // 2
    n_tp, n_ex = lax.axis_size("tp"), lax.axis_size("ex")
    count, width = tokens.shape
    w_gate, w_up, w_down = gate_weight[0], up_weight[0], down_weight[0]
    inner = w_down.shape[0]

    def partial_sums(rows):
        parts = [jnp.dot(rows, w, preferred_element_type=f32) for w in (w_gate, w_up)]
        part = jnp.concatenate(parts, axis=1)
        sent = part.astype(bf16)
        return part, sent, [shift(sent, "ex", s) for s in range(1, n_ex)]

    def partial_out(part, others):
        for other in others:
            part = part + other.astype(f32)
        hidden = (jax.nn.silu(part[:, :inner]) * part[:, inner:]).astype(bf16)
        out = jnp.dot(hidden, w_down, preferred_element_type=f32)
        kept = out.shape[0] // 2
        return out[:kept] + swap_half(out[kept:].astype(bf16)).astype(f32)

    held = copied(tokens)
    blocks = [held] + [shift(tokens, "tp", t) for t in (n_tp - 1, *range(1, n_tp - 1))]
    first, rest = jnp.concatenate(blocks[:2], axis=0), jnp.concatenate(blocks[2:], axis=0)
    far_first = [shift_expert(first, s) for s in range(1, experts)]
    far_rest = [shift_expert(rest, s) for s in range(1, experts)]
    near = jnp.concatenate([first, rest], axis=0)
    near = jnp.concatenate([near, swap_half(near)], axis=0)
    near_part, near_sent, near_others = partial_sums(near)
    far = []
    for one, two in zip(far_first, far_rest):
        far += [one, after(two, near_sent)]
    far = jnp.concatenate(far, axis=0)
    far = jnp.concatenate([far, swap_half(far)], axis=0)
    far_part, far_sent, far_others = partial_sums(far)
    places = (0, n_tp - 1, *range(1, n_tp - 1))
    near_out = partial_out(near_part, [after(other, far_sent) for other in near_others])
    near_out = near_out.reshape(n_tp, count, width)
    near_sent = near_out[1:].astype(bf16)
    pieces = [near_out[0]] + [shift(near_sent[i], "tp", -t) for i, t in enumerate(places[1:])]
    far_out = partial_out(far_part, [after(other, near_sent) for other in far_others])
    far_out = far_out.reshape(experts - 1, n_tp, count, width).astype(bf16)
    for s in range(1, experts):
        pieces += [shift_expert(far_out[experts - 1 - s, i], s, -t) for i, t in enumerate(places)]
    return mix(expert_ids, gate_levels, pieces, n_tp, experts)


def solution(mesh):
    return jax.shard_map(
        per_device,
        mesh=mesh,
        in_specs=(
            P(("grp", "tp"), "ex"),
            P(("grp", "tp"), None),
            P(("grp", "tp"), None),
            P("grp", "ex", "tp"),
            P("grp", "ex", "tp"),
            P("grp", "tp", "ex"),
        ),
        out_specs=P(("grp", "tp"), "ex"),
        check_vma=False,
    )
```

time: 49.8 us -> 42.5 us (0.85)
  waiting for transfers between devices: 22 us -> 15 us
  other arithmetic: 5 us -> 0.22 us
  starting transfers between devices: 18 us -> 22.5 us
  matrix products: 4.1 us -> 2.59 us
  Pallas kernels: 0 us -> 0.75 us
  local copies, waits for them, and re-layouts: 0.29 us -> 1.02 us
    ppermute x2 -> x6, starting transfers between devices: 2.15 us -> 9.27 us  [shift_expert(): return lax.ppermute(value, ('grp', 'tp'), pairs)]
    ppermute x8, waiting for transfers between devices: 12.9 us -> 7.6 us  [shift(): lax.ppermute(value, axis, [(i, (i + by) % size) for i in range(size)])]
    ppermute x8, starting transfers between devices: 15.2 us -> 13 us  [shift(): lax.ppermute(value, axis, [(i, (i + by) % size) for i in range(size)])]
    another operation x4 -> x1, other arithmetic: 2.19 us -> 0.06 us
    dot_general x6, matrix products: 4.1 us -> 2.59 us  [the longest x4 1.76 us: partial_sums(): jnp.dot(rows, w, preferred_element_type=f32)]
    ppermute x2 -> x6, waiting for transfers between devices: 7.1 us -> 5.92 us  [shift_expert(): return lax.ppermute(value, ('grp', 'tp'), pairs)]
    unnamed x1 -> x0, other arithmetic: 0.83 us -> none
    concatenate x2 -> x4, other arithmetic: 0.85 us -> 0.06 us  [the longest x1 0.02 us: per_device(): near = jnp.concatenate([first, rest], axis=0)]
  transfers between devices with their start and end apart: 14 -> 18, of which waited for: 9 -> 9; matrix products, arithmetic and copies ran while one was open for 7% -> 5% of each run, Pallas kernels for 0% -> 0%
where the time goes in v2:
time: 42.5 us; the launch traced here: 42.3 us
  starting transfers between devices  22.5 us (53%)
  waiting for transfers between devices  15 us (35%)
  matrix products  2.59 us (6%)
  local copies, waits for them, and re-layouts  1.02 us (2%)
  Pallas kernels  0.75 us (2%)
    ppermute x8, starting transfers between devices, shift(): lax.ppermute(value, axis, [(i, (i + by) % size) for i in range(size)])  13 us
    ppermute x6, starting transfers between devices, shift_expert(): return lax.ppermute(value, ('grp', 'tp'), pairs)  9.27 us
    ppermute x8, waiting for transfers between devices, shift(): lax.ppermute(value, axis, [(i, (i + by) % size) for i in range(size)])  7.6 us
    ppermute x6, waiting for transfers between devices, shift_expert(): return lax.ppermute(value, ('grp', 'tp'), pairs)  5.92 us
    dot_general x4, matrix products, partial_sums(): jnp.dot(rows, w, preferred_element_type=f32)  1.76 us
    ppermute x4, waiting for transfers between devices, swap_half(): lax.ppermute(value, 'grp', [(i, i ^ 1) for i in range(lax.axis_size('grp'...  1.44 us
    unnamed x16, local copies, waits for them, and re-layouts  0.9 us
  transfers between devices with their start and end apart: 18, of which 9 were waited for; matrix products, arithmetic and copies ran while one was open for 5% of the time, Pallas kernels for 0%

profile of v2, /device:TPU:0, one launch (start us, length us, event | category | flops | bytes accessed | tf_op | source)
XLA Modules:
  0.0 42.3 jit_solution(12292089906570591741)
XLA Ops:
  0.0 0.0 copy-start
  0.0 5.0 %collective-permute-start = (bf16[8,3584]{1,0:T(8,128)(2,1)}, bf16[8,3584]{1,0:T(8,128)(2,1)S(1)}, u32[]{:S(2)}, u32[]{:S(2)}) collective-permute-start(bf16[8,3584]{1,0:T(8,128)(2,1)} %from_ref.1), channel_id=1, source_target_pairs={{0,6},{2,0},{4,2},{6,4},{1,7},{3,1},{5,3},{7,5},{8,14},{10,8},{12,... | collective-permute-start | bytes 172040 | tf_op jit(solution)/shard_map/ppermute | solution.py:16
  5.1 0.0 collective-permute-start.2
  5.1 1.0 %collective-permute-start.1 = (bf16[8,3584]{1,0:T(8,128)(2,1)}, bf16[8,3584]{1,0:T(8,128)(2,1)S(1)}, u32[]{:S(2)}, u32[]{:S(2)}) collective-permute-start(bf16[8,3584]{1,0:T(8,128)(2,1)} %from_ref.1), channel_id=1, source_target_pairs={{0,2},{2,4},{4,6},{6,0},{1,3},{3,5},{5,7},{7,1},{8,10},{10,12},{12... | collective-permute-start | bytes 172040 | tf_op jit(solution)/shard_map/ppermute | solution.py:16
  6.1 0.0 copy-start.1
  6.1 0.9 %copy-done.1 = bf16[8,3584]{1,0:T(8,128)(2,1)S(1)} copy-done((bf16[8,3584]{1,0:T(8,128)(2,1)S(1)}, bf16[8,3584]{1,0:T(8,128)(2,1)}, u32[]{:S(2)}) %copy-start.1) | copy-done | bytes 57368
  6.9 0.0 copy-start.4
  6.9 0.8 %collective-permute-done = bf16[8,3584]{1,0:T(8,128)(2,1)S(1)} collective-permute-done((bf16[8,3584]{1,0:T(8,128)(2,1)}, bf16[8,3584]{1,0:T(8,128)(2,1)S(1)}, u32[]{:S(2)}, u32[]{:S(2)}) %collective-permute-start) | collective-permute-done | bytes 57376 | tf_op jit(solution)/shard_map/ppermute | solution.py:16
  7.7 1.6 %collective-permute-start.5 = (bf16[16,3584]{1,0:T(8,128)(2,1)S(1)}, bf16[16,3584]{1,0:T(8,128)(2,1)S(1)}, u32[]{:S(2)}, u32[]{:S(2)}) collective-permute-start(bf16[16,3584]{1,0:T(8,128)(2,1)S(1)} %pad_maximum_fusion.7), channel_id=1, source_target_pairs={{0,16},{2,18},{4,20},{6,22},{8,24},{10,26},{12,28},{14,30},{16,0},... | collective-permute-start | bytes 344072 | tf_op jit(solution)/shard_map/ppermute | solution.py:26
  9.3 1.2 %collective-permute-done.2 = bf16[8,3584]{1,0:T(8,128)(2,1)S(1)} collective-permute-done((bf16[8,3584]{1,0:T(8,128)(2,1)}, bf16[8,3584]{1,0:T(8,128)(2,1)S(1)}, u32[]{:S(2)}, u32[]{:S(2)}) %collective-permute-start.2) | collective-permute-done | bytes 57376 | tf_op jit(solution)/shard_map/ppermute | solution.py:16
  10.4 0.8 %collective-permute-done.1 = bf16[8,3584]{1,0:T(8,128)(2,1)S(1)} collective-permute-done((bf16[8,3584]{1,0:T(8,128)(2,1)}, bf16[8,3584]{1,0:T(8,128)(2,1)S(1)}, u32[]{:S(2)}, u32[]{:S(2)}) %collective-permute-start.1) | collective-permute-done | bytes 57376 | tf_op jit(solution)/shard_map/ppermute | solution.py:16
  11.3 0.0 copy-start.5
  11.3 1.6 %collective-permute-start.6 = (bf16[16,3584]{1,0:T(8,128)(2,1)S(1)}, bf16[16,3584]{1,0:T(8,128)(2,1)S(1)}, u32[]{:S(2)}, u32[]{:S(2)}) collective-permute-start(bf16[16,3584]{1,0:T(8,128)(2,1)S(1)} %pad_maximum_fusion.8), channel_id=1, source_target_pairs={{0,16},{2,18},{4,20},{6,22},{8,24},{10,26},{12,28},{14,30},{16,0},... | collective-permute-start | bytes 344072 | tf_op jit(solution)/shard_map/ppermute | solution.py:26
  12.8 0.1 collective-permute-start.3
  13.0 1.4 %collective-permute-done.3 = bf16[32,3584]{1,0:T(8,128)(2,1)S(1)} collective-permute-done((bf16[32,3584]{1,0:T(8,128)(2,1)S(1)}, bf16[32,3584]{1,0:T(8,128)(2,1)S(1)}, u32[]{:S(2)}, u32[]{:S(2)}) %collective-permute-start.3) | collective-permute-done | bytes 229408 | tf_op jit(solution)/shard_map/ppermute | solution.py:30
  14.4 0.0 copy-done.4
  14.4 0.4 %fusion.6 = f32[64,256]{1,0:T(8,128)S(1)} fusion(bf16[64,3584]{1,0:T(8,128)(2,1)S(1)} %constant_dynamic-update-slice_fusion, bf16[1,3584,256]{2,1,0:T(8,128)(2,1)S(1)} %copy-done.4), kind=kOutput, calls=%fused_computation.6 | convolution fusion | flops 117440512 | bytes 2359296 | tf_op jit(solution)/shard_map/dot_general | solution.py:98
  14.9 0.0 copy-done.5
  14.9 0.4 %fusion.10 = f32[64,256]{1,0:T(8,128)S(1)} fusion(bf16[64,3584]{1,0:T(8,128)(2,1)S(1)} %constant_dynamic-update-slice_fusion, bf16[1,3584,256]{2,1,0:T(8,128)(2,1)S(1)} %copy-done.5), kind=kOutput, calls=%fused_computation.10 | convolution fusion | flops 117440512 | bytes 2359296 | tf_op jit(solution)/shard_map/dot_general | solution.py:98
  15.3 0.8 %collective-permute-done.6.refs_0_ = bf16[16,3584]{1,0:T(8,128)(2,1)S(1)} collective-permute-done((bf16[16,3584]{1,0:T(8,128)(2,1)S(1)}, bf16[16,3584]{1,0:T(8,128)(2,1)S(1)}, u32[]{:S(2)}, u32[]{:S(2)}) %collective-permute-start.6) | collective-permute-done | bytes 114720 | tf_op jit(solution)/shard_map/ppermute | solution.py:26
  16.1 0.0 collective-permute-done.5
  16.1 0.1 collective-permute-start.7
  16.2 1.6 %collective-permute-start.4 = (bf16[64,512]{1,0:T(8,128)(2,1)S(1)}, bf16[64,512]{1,0:T(8,128)(2,1)S(1)}, u32[]{:S(2)}, u32[]{:S(2)}) collective-permute-start(bf16[64,512]{1,0:T(8,128)(2,1)S(1)} %fusion.15.refs_1_), channel_id=1, source_target_pairs={{0,1},{1,0},{2,3},{3,2},{4,5},{5,4},{6,7},{7,6},{8,9},{9,8},{10,11... | collective-permute-start | bytes 196616 | tf_op jit(solution)/shard_map/ppermute | solution.py:16
  17.8 0.0 collective-permute-done.7
  17.8 0.4 %fusion.4 = f32[64,256]{1,0:T(8,128)S(1)} fusion(bf16[1,3584,256]{2,1,0:T(8,128)(2,1)S(1)} %copy-done.4, bf16[32,3584]{1,0:T(8,128)(2,1)S(1)} %collective-permute-done.7, bf16[16,3584]{1,0:T(8,128)(2,1)S(1)} %shard_map.65, bf16[16,3584]{1,0:T(8,128)(2,1)S(1)} %collective-permute-done.5), kind=kOutput, calls=%fused_computation.4 | convolution fusion | flops 118816768 | bytes 2359296 | tf_op jit(solution)/shard_map/dot_general | solution.py:98
  18.3 0.4 %fusion.8 = f32[64,256]{1,0:T(8,128)S(1)} fusion(bf16[1,3584,256]{2,1,0:T(8,128)(2,1)S(1)} %copy-done.5, bf16[32,3584]{1,0:T(8,128)(2,1)S(1)} %collective-permute-done.7, bf16[16,3584]{1,0:T(8,128)(2,1)S(1)} %shard_map.65, bf16[16,3584]{1,0:T(8,128)(2,1)S(1)} %collective-permute-done.5), kind=kOutput, calls=%fused_computation.8 | convolution fusion | flops 118816768 | bytes 2359296 | tf_op jit(solution)/shard_map/dot_general | solution.py:98
  18.7 2.0 %collective-permute-done.4.refs_0_ = bf16[64,512]{1,0:T(8,128)(2,1)S(1)} collective-permute-done((bf16[64,512]{1,0:T(8,128)(2,1)S(1)}, bf16[64,512]{1,0:T(8,128)(2,1)S(1)}, u32[]{:S(2)}, u32[]{:S(2)}) %collective-permute-start.4) | collective-permute-done | bytes 65568 | tf_op jit(solution)/shard_map/ppermute | solution.py:16
  20.8 0.0 copy-done
  20.8 0.4 fusion.2
  21.2 0.1 collective-permute-start.8
  21.3 1.6 %collective-permute-start.12 = (bf16[64,512]{1,0:T(8,128)(2,1)S(1)}, bf16[64,512]{1,0:T(8,128)(2,1)S(1)}, u32[]{:S(2)}, u32[]{:S(2)}) collective-permute-start(bf16[64,512]{1,0:T(8,128)(2,1)S(1)} %fusion.14.refs_1_), channel_id=1, source_target_pairs={{0,1},{1,0},{2,3},{3,2},{4,5},{5,4},{6,7},{7,6},{8,9},{9,8},{10,11... | collective-permute-start | bytes 196616 | tf_op jit(solution)/shard_map/ppermute | solution.py:16
  22.9 0.0 collective-permute-done.8
  22.9 0.1 fusion.26
  23.0 2.8 %collective-permute-done.12.refs_0_ = bf16[64,512]{1,0:T(8,128)(2,1)S(1)} collective-permute-done((bf16[64,512]{1,0:T(8,128)(2,1)S(1)}, bf16[64,512]{1,0:T(8,128)(2,1)S(1)}, u32[]{:S(2)}, u32[]{:S(2)}) %collective-permute-start.12) | collective-permute-done | bytes 65568 | tf_op jit(solution)/shard_map/ppermute | solution.py:16
  25.8 0.4 fusion
  26.2 0.0 copy-start.2
  26.3 0.0 copy-start.3
  26.3 0.1 collective-permute-start.13
  26.4 1.7 %collective-permute-start.11 = (bf16[8,3584]{1,0:T(8,128)(2,1)S(1)}, bf16[8,3584]{1,0:T(8,128)(2,1)S(1)}, u32[]{:S(2)}, u32[]{:S(2)}) collective-permute-start(bf16[8,3584]{1,0:T(8,128)(2,1)S(1)} %get-tuple-element.11), channel_id=1, source_target_pairs={{0,4},{2,6},{4,0},{6,2},{1,5},{3,7},{5,1},{7,3},{8,12},{10,14},{12... | collective-permute-start | bytes 172040 | tf_op jit(solution)/shard_map/ppermute | solution.py:16
  28.1 1.3 %collective-permute-start.10 = (bf16[8,3584]{1,0:T(8,128)(2,1)S(1)}, bf16[8,3584]{1,0:T(8,128)(2,1)S(1)}, u32[]{:S(2)}, u32[]{:S(2)}) collective-permute-start(bf16[8,3584]{1,0:T(8,128)(2,1)S(1)} %get-tuple-element.12), channel_id=1, source_target_pairs={{0,6},{2,0},{4,2},{6,4},{1,7},{3,1},{5,3},{7,5},{8,14},{10,8},{12,... | collective-permute-start | bytes 172040 | tf_op jit(solution)/shard_map/ppermute | solution.py:16
  29.5 0.7 %collective-permute-start.9 = (bf16[8,3584]{1,0:T(8,128)(2,1)S(1)}, bf16[8,3584]{1,0:T(8,128)(2,1)S(1)}, u32[]{:S(2)}, u32[]{:S(2)}) collective-permute-start(bf16[8,3584]{1,0:T(8,128)(2,1)S(1)} %get-tuple-element.13), channel_id=1, source_target_pairs={{0,2},{2,4},{4,6},{6,0},{1,3},{3,5},{5,7},{7,1},{8,10},{10,12},{12... | collective-permute-start | bytes 172040 | tf_op jit(solution)/shard_map/ppermute | solution.py:16
  30.1 0.0 collective-permute-done.13
  30.2 2.3 %collective-permute-start.17 = (bf16[8,3584]{1,0:T(8,128)(2,1)S(1)}, bf16[8,3584]{1,0:T(8,128)(2,1)S(1)}, u32[]{:S(2)}, u32[]{:S(2)}) collective-permute-start(bf16[8,3584]{1,0:T(8,128)(2,1)S(1)} %get-tuple-element.7), channel_id=1, source_target_pairs={{0,20},{2,22},{4,16},{6,18},{8,28},{10,30},{12,24},{14,26},{16,4},... | collective-permute-start | bytes 172040 | tf_op jit(solution)/shard_map/ppermute | solution.py:26
  32.5 2.2 %collective-permute-start.16 = (bf16[8,3584]{1,0:T(8,128)(2,1)S(1)}, bf16[8,3584]{1,0:T(8,128)(2,1)S(1)}, u32[]{:S(2)}, u32[]{:S(2)}) collective-permute-start(bf16[8,3584]{1,0:T(8,128)(2,1)S(1)} %get-tuple-element.8), channel_id=1, source_target_pairs={{0,22},{2,16},{4,18},{6,20},{8,30},{10,24},{12,26},{14,28},{16,6},... | collective-permute-start | bytes 172040 | tf_op jit(solution)/shard_map/ppermute | solution.py:26
  34.7 0.0 collective-permute-done.11.refs_3_
  34.7 0.8 %collective-permute-start.15 = (bf16[8,3584]{1,0:T(8,128)(2,1)S(1)}, bf16[8,3584]{1,0:T(8,128)(2,1)S(1)}, u32[]{:S(2)}, u32[]{:S(2)}) collective-permute-start(bf16[8,3584]{1,0:T(8,128)(2,1)S(1)} %get-tuple-element.9), channel_id=1, source_target_pairs={{0,18},{2,20},{4,22},{6,16},{8,26},{10,28},{12,30},{14,24},{16,2},... | collective-permute-start | bytes 172040 | tf_op jit(solution)/shard_map/ppermute | solution.py:26
  35.4 0.0 collective-permute-done.10.refs_2_
  35.4 1.0 %collective-permute-start.14 = (bf16[8,3584]{1,0:T(8,128)(2,1)S(1)}, bf16[8,3584]{1,0:T(8,128)(2,1)S(1)}, u32[]{:S(2)}, u32[]{:S(2)}) collective-permute-start(bf16[8,3584]{1,0:T(8,128)(2,1)S(1)} %get-tuple-element.10), channel_id=1, source_target_pairs={{0,16},{2,18},{4,20},{6,22},{8,24},{10,26},{12,28},{14,30},{16,0},... | collective-permute-start | bytes 172040 | tf_op jit(solution)/shard_map/ppermute | solution.py:26
  36.4 0.0 collective-permute-done.9.refs_1_
  36.4 2.5 %collective-permute-done.17.refs_7_ = bf16[8,3584]{1,0:T(8,128)(2,1)S(1)} collective-permute-done((bf16[8,3584]{1,0:T(8,128)(2,1)S(1)}, bf16[8,3584]{1,0:T(8,128)(2,1)S(1)}, u32[]{:S(2)}, u32[]{:S(2)}) %collective-permute-start.17) | collective-permute-done | bytes 57376 | tf_op jit(solution)/shard_map/ppermute | solution.py:26
  38.9 0.0 collective-permute-done.16.refs_6_
  38.9 2.6 %collective-permute-done.15.refs_5_ = bf16[8,3584]{1,0:T(8,128)(2,1)S(1)} collective-permute-done((bf16[8,3584]{1,0:T(8,128)(2,1)S(1)}, bf16[8,3584]{1,0:T(8,128)(2,1)S(1)}, u32[]{:S(2)}, u32[]{:S(2)}) %collective-permute-start.15) | collective-permute-done | bytes 57376 | tf_op jit(solution)/shard_map/ppermute | solution.py:26
  41.5 0.0 collective-permute-done.14.refs_4_
  41.5 0.0 copy-done.2
  41.6 0.0 copy-done.3
  41.6 0.7 %shard_map.68 = bf16[8,3584]{1,0:T(8,128)(2,1)} custom-call(s32[1,8]{1,0:T(1,128)S(1)} %bitcast.31, s32[1,8]{1,0:T(1,128)S(1)} %bitcast.32, f32[8,3584]{1,0:T(8,128)S(1)} %slice.83.refs_0_, bf16[8,3584]{1,0:T(8,128)(2,1)S(1)} %collective-permute-done.9.refs_1_, bf16[8,3584]{1,0:T(8,128)(2,1)S(1)} %collective-permute-done.10.refs_2_, ...), custom_call_target="tpu_custom_call" | custom-call | tf_op jit(solution)/shard_map/pallas_call | solution.py:82
  (24 shorter events, 0.3 us)
Async XLA Ops:
  0.0 20.8 %copy-start = (bf16[1,256,3584]{2,1,0:T(8,128)(2,1)S(1)}, bf16[1,256,3584]{2,1,0:T(8,128)(2,1)}, u32[]{:S(2)}) copy-start(bf16[1,256,3584]{2,1,0:T(8,128)(2,1)} %param.11) | copy-start | bytes 5505028
  0.0 7.7 %collective-permute-start = (bf16[8,3584]{1,0:T(8,128)(2,1)}, bf16[8,3584]{1,0:T(8,128)(2,1)S(1)}, u32[]{:S(2)}, u32[]{:S(2)}) collective-permute-start(bf16[8,3584]{1,0:T(8,128)(2,1)} %from_ref.1), channel_id=1, source_target_pairs={{0,6},{2,0},{4,2},{6,4},{1,7},{3,1},{5,3},{7,5},{8,14},{10,8},{12,... | collective-permute-start | bytes 172040 | tf_op jit(solution)/shard_map/ppermute | solution.py:16
  5.1 5.4 %collective-permute-start.2 = (bf16[8,3584]{1,0:T(8,128)(2,1)}, bf16[8,3584]{1,0:T(8,128)(2,1)S(1)}, u32[]{:S(2)}, u32[]{:S(2)}) collective-permute-start(bf16[8,3584]{1,0:T(8,128)(2,1)} %from_ref.1), channel_id=1, source_target_pairs={{0,4},{2,6},{4,0},{6,2},{1,5},{3,7},{5,1},{7,3},{8,12},{10,14},{12... | collective-permute-start | bytes 172040 | tf_op jit(solution)/shard_map/ppermute | solution.py:16
  5.1 6.2 %collective-permute-start.1 = (bf16[8,3584]{1,0:T(8,128)(2,1)}, bf16[8,3584]{1,0:T(8,128)(2,1)S(1)}, u32[]{:S(2)}, u32[]{:S(2)}) collective-permute-start(bf16[8,3584]{1,0:T(8,128)(2,1)} %from_ref.1), channel_id=1, source_target_pairs={{0,2},{2,4},{4,6},{6,0},{1,3},{3,5},{5,7},{7,1},{8,10},{10,12},{12... | collective-permute-start | bytes 172040 | tf_op jit(solution)/shard_map/ppermute | solution.py:16
  6.1 0.9 %copy-start.1 = (bf16[8,3584]{1,0:T(8,128)(2,1)S(1)}, bf16[8,3584]{1,0:T(8,128)(2,1)}, u32[]{:S(2)}) copy-start(bf16[8,3584]{1,0:T(8,128)(2,1)} %from_ref.1) | copy-start | bytes 172036
  6.9 7.5 %copy-start.4 = (bf16[1,3584,256]{2,1,0:T(8,128)(2,1)S(1)}, bf16[1,3584,256]{2,1,0:T(8,128)(2,1)}, u32[]{:S(2)}) copy-start(bf16[1,3584,256]{2,1,0:T(8,128)(2,1)} %param.10) | copy-start | bytes 5505028
  7.7 8.4 %collective-permute-start.5 = (bf16[16,3584]{1,0:T(8,128)(2,1)S(1)}, bf16[16,3584]{1,0:T(8,128)(2,1)S(1)}, u32[]{:S(2)}, u32[]{:S(2)}) collective-permute-start(bf16[16,3584]{1,0:T(8,128)(2,1)S(1)} %pad_maximum_fusion.7), channel_id=1, source_target_pairs={{0,16},{2,18},{4,20},{6,22},{8,24},{10,26},{12,28},{14,30},{16,0},... | collective-permute-start | bytes 344072 | tf_op jit(solution)/shard_map/ppermute | solution.py:26
  11.3 3.6 %copy-start.5 = (bf16[1,3584,256]{2,1,0:T(8,128)(2,1)S(1)}, bf16[1,3584,256]{2,1,0:T(8,128)(2,1)}, u32[]{:S(2)}) copy-start(bf16[1,3584,256]{2,1,0:T(8,128)(2,1)} %param.9) | copy-start | bytes 5505028
  11.3 4.9 %collective-permute-start.6 = (bf16[16,3584]{1,0:T(8,128)(2,1)S(1)}, bf16[16,3584]{1,0:T(8,128)(2,1)S(1)}, u32[]{:S(2)}, u32[]{:S(2)}) collective-permute-start(bf16[16,3584]{1,0:T(8,128)(2,1)S(1)} %pad_maximum_fusion.8), channel_id=1, source_target_pairs={{0,16},{2,18},{4,20},{6,22},{8,24},{10,26},{12,28},{14,30},{16,0},... | collective-permute-start | bytes 344072 | tf_op jit(solution)/shard_map/ppermute | solution.py:26
  12.8 1.6 %collective-permute-start.3 = (bf16[32,3584]{1,0:T(8,128)(2,1)S(1)}, bf16[32,3584]{1,0:T(8,128)(2,1)S(1)}, u32[]{:S(2)}, u32[]{:S(2)}) collective-permute-start(bf16[32,3584]{1,0:T(8,128)(2,1)S(1)} %pad_maximum_fusion.1), channel_id=1, source_target_pairs={{0,8},{8,0},{16,24},{24,16},{1,9},{9,1},{17,25},{25,17},{2,10},{10... | collective-permute-start | bytes 688136 | tf_op jit(solution)/shard_map/ppermute | solution.py:30
  16.1 1.7 %collective-permute-start.7 = (bf16[32,3584]{1,0:T(8,128)(2,1)S(1)}, bf16[32,3584]{1,0:T(8,128)(2,1)S(1)}, u32[]{:S(2)}, u32[]{:S(2)}) collective-permute-start(bf16[32,3584]{1,0:T(8,128)(2,1)S(1)} %pad_maximum_fusion.2), channel_id=1, source_target_pairs={{0,8},{8,0},{16,24},{24,16},{1,9},{9,1},{17,25},{25,17},{2,10},{10... | collective-permute-start | bytes 688136 | tf_op jit(solution)/shard_map/ppermute | solution.py:30
  16.2 4.5 %collective-permute-start.4 = (bf16[64,512]{1,0:T(8,128)(2,1)S(1)}, bf16[64,512]{1,0:T(8,128)(2,1)S(1)}, u32[]{:S(2)}, u32[]{:S(2)}) collective-permute-start(bf16[64,512]{1,0:T(8,128)(2,1)S(1)} %fusion.15.refs_1_), channel_id=1, source_target_pairs={{0,1},{1,0},{2,3},{3,2},{4,5},{5,4},{6,7},{7,6},{8,9},{9,8},{10,11... | collective-permute-start | bytes 196616 | tf_op jit(solution)/shard_map/ppermute | solution.py:16
  21.2 1.7 %collective-permute-start.8 = (bf16[32,3584]{1,0:T(8,128)(2,1)S(1)}, bf16[32,3584]{1,0:T(8,128)(2,1)S(1)}, u32[]{:S(2)}, u32[]{:S(2)}) collective-permute-start(bf16[32,3584]{1,0:T(8,128)(2,1)S(1)} %slice.122), channel_id=1, source_target_pairs={{0,8},{8,0},{16,24},{24,16},{1,9},{9,1},{17,25},{25,17},{2,10},{10... | collective-permute-start | bytes 688136 | tf_op jit(solution)/shard_map/ppermute | solution.py:30
  21.3 4.5 %collective-permute-start.12 = (bf16[64,512]{1,0:T(8,128)(2,1)S(1)}, bf16[64,512]{1,0:T(8,128)(2,1)S(1)}, u32[]{:S(2)}, u32[]{:S(2)}) collective-permute-start(bf16[64,512]{1,0:T(8,128)(2,1)S(1)} %fusion.14.refs_1_), channel_id=1, source_target_pairs={{0,1},{1,0},{2,3},{3,2},{4,5},{5,4},{6,7},{7,6},{8,9},{9,8},{10,11... | collective-permute-start | bytes 196616 | tf_op jit(solution)/shard_map/ppermute | solution.py:16
  26.2 15.3 %copy-start.2 = (s32[8,1]{0,1:T(1,128)S(1)}, s32[8,1]{0,1:T(1,128)}, u32[]{:S(2)}) copy-start(s32[8,1]{0,1:T(1,128)} %param.7) | copy-start | bytes 100
  26.3 15.3 %copy-start.3 = (s32[8,1]{0,1:T(1,128)S(1)}, s32[8,1]{0,1:T(1,128)}, u32[]{:S(2)}) copy-start(s32[8,1]{0,1:T(1,128)} %param.8) | copy-start | bytes 100
  26.3 3.8 %collective-permute-start.13 = (bf16[32,3584]{1,0:T(8,128)(2,1)S(1)}, bf16[32,3584]{1,0:T(8,128)(2,1)S(1)}, u32[]{:S(2)}, u32[]{:S(2)}) collective-permute-start(bf16[32,3584]{1,0:T(8,128)(2,1)S(1)} %slice.121), channel_id=1, source_target_pairs={{0,8},{8,0},{16,24},{24,16},{1,9},{9,1},{17,25},{25,17},{2,10},{10... | collective-permute-start | bytes 688136 | tf_op jit(solution)/shard_map/ppermute | solution.py:30
  26.4 8.3 %collective-permute-start.11 = (bf16[8,3584]{1,0:T(8,128)(2,1)S(1)}, bf16[8,3584]{1,0:T(8,128)(2,1)S(1)}, u32[]{:S(2)}, u32[]{:S(2)}) collective-permute-start(bf16[8,3584]{1,0:T(8,128)(2,1)S(1)} %get-tuple-element.11), channel_id=1, source_target_pairs={{0,4},{2,6},{4,0},{6,2},{1,5},{3,7},{5,1},{7,3},{8,12},{10,14},{12... | collective-permute-start | bytes 172040 | tf_op jit(solution)/shard_map/ppermute | solution.py:16
  28.1 7.3 %collective-permute-start.10 = (bf16[8,3584]{1,0:T(8,128)(2,1)S(1)}, bf16[8,3584]{1,0:T(8,128)(2,1)S(1)}, u32[]{:S(2)}, u32[]{:S(2)}) collective-permute-start(bf16[8,3584]{1,0:T(8,128)(2,1)S(1)} %get-tuple-element.12), channel_id=1, source_target_pairs={{0,6},{2,0},{4,2},{6,4},{1,7},{3,1},{5,3},{7,5},{8,14},{10,8},{12,... | collective-permute-start | bytes 172040 | tf_op jit(solution)/shard_map/ppermute | solution.py:16
  29.5 7.0 %collective-permute-start.9 = (bf16[8,3584]{1,0:T(8,128)(2,1)S(1)}, bf16[8,3584]{1,0:T(8,128)(2,1)S(1)}, u32[]{:S(2)}, u32[]{:S(2)}) collective-permute-start(bf16[8,3584]{1,0:T(8,128)(2,1)S(1)} %get-tuple-element.13), channel_id=1, source_target_pairs={{0,2},{2,4},{4,6},{6,0},{1,3},{3,5},{5,7},{7,1},{8,10},{10,12},{12... | collective-permute-start | bytes 172040 | tf_op jit(solution)/shard_map/ppermute | solution.py:16
  30.2 8.7 %collective-permute-start.17 = (bf16[8,3584]{1,0:T(8,128)(2,1)S(1)}, bf16[8,3584]{1,0:T(8,128)(2,1)S(1)}, u32[]{:S(2)}, u32[]{:S(2)}) collective-permute-start(bf16[8,3584]{1,0:T(8,128)(2,1)S(1)} %get-tuple-element.7), channel_id=1, source_target_pairs={{0,20},{2,22},{4,16},{6,18},{8,28},{10,30},{12,24},{14,26},{16,4},... | collective-permute-start | bytes 172040 | tf_op jit(solution)/shard_map/ppermute | solution.py:26
  32.5 6.4 %collective-permute-start.16 = (bf16[8,3584]{1,0:T(8,128)(2,1)S(1)}, bf16[8,3584]{1,0:T(8,128)(2,1)S(1)}, u32[]{:S(2)}, u32[]{:S(2)}) collective-permute-start(bf16[8,3584]{1,0:T(8,128)(2,1)S(1)} %get-tuple-element.8), channel_id=1, source_target_pairs={{0,22},{2,16},{4,18},{6,20},{8,30},{10,24},{12,26},{14,28},{16,6},... | collective-permute-start | bytes 172040 | tf_op jit(solution)/shard_map/ppermute | solution.py:26
  34.7 6.9 %collective-permute-start.15 = (bf16[8,3584]{1,0:T(8,128)(2,1)S(1)}, bf16[8,3584]{1,0:T(8,128)(2,1)S(1)}, u32[]{:S(2)}, u32[]{:S(2)}) collective-permute-start(bf16[8,3584]{1,0:T(8,128)(2,1)S(1)} %get-tuple-element.9), channel_id=1, source_target_pairs={{0,18},{2,20},{4,22},{6,16},{8,26},{10,28},{12,30},{14,24},{16,2},... | collective-permute-start | bytes 172040 | tf_op jit(solution)/shard_map/ppermute | solution.py:26
  35.4 6.1 %collective-permute-start.14 = (bf16[8,3584]{1,0:T(8,128)(2,1)S(1)}, bf16[8,3584]{1,0:T(8,128)(2,1)S(1)}, u32[]{:S(2)}, u32[]{:S(2)}) collective-permute-start(bf16[8,3584]{1,0:T(8,128)(2,1)S(1)} %get-tuple-element.10), channel_id=1, source_target_pairs={{0,16},{2,18},{4,20},{6,22},{8,24},{10,26},{12,28},{14,30},{16,0},... | collective-permute-start | bytes 172040 | tf_op jit(solution)/shard_map/ppermute | solution.py:26
